TPU v7x, 32 devices: a whole 2x2x4 slice. The times are simulated.
32 devices in a mesh: dp: 16 (over z, y, x), tensor: 2 (over core).
Axes of the slice: x: 2, y: 2, z: 4, core: 2. Of those that a mesh axis runs over, the one named last changes fastest.
Arguments:
- inputs: bfloat16 [2, 8192, 1024], P(None, ('dp', 'tensor')), may hold values from -6 to 6
- lengths: int32 [2, 16, 8], P(None, 'dp'), may hold values from 0 to 512, as said below
- query_weight: bfloat16 [1024, 1024], P(None, 'tensor'), may hold values from -0.1875 to 0.1875
- key_weight: bfloat16 [1024, 1024], P(None, 'tensor'), may hold values from -0.1875 to 0.1875
- value_weight: bfloat16 [1024, 1024], P(None, 'tensor'), may hold values from -0.1875 to 0.1875
- output_weight: bfloat16 [1024, 1024], P('tensor'), may hold values from -0.1875 to 0.1875
- inner_weight: bfloat16 [1024, 4096], P(None, 'tensor'), may hold values from -0.1875 to 0.1875
- outer_weight: bfloat16 [4096, 1024], P('tensor'), may hold values from -0.09375 to 0.09375
- entry_gain: float32 [1024], replicated, may hold values from 0.25 to 1.75
- entry_bias: float32 [1024], replicated, may hold values from -3 to 3
- merge_gain: float32 [1024], replicated, may hold values from 0.25 to 1.75
- merge_bias: float32 [1024], replicated, may hold values from -3 to 3
- inlet_gain: float32 [1024], replicated, may hold values from 0.25 to 1.75
- inlet_bias: float32 [1024], replicated, may hold values from -3 to 3
- outlet_gain: float32 [1024], replicated, may hold values from 0.25 to 1.75
- outlet_bias: float32 [1024], replicated, may hold values from -3 to 3
- cotangent: bfloat16 [2, 8192, 1024], P(None, ('dp', 'tensor')), may hold values from -6 to 6
Outputs:
- outputs: bfloat16 [2, 8192, 1024], P(None, ('dp', 'tensor'))
- input_grad: bfloat16 [2, 8192, 1024], P(None, ('dp', 'tensor'))
- query_grad: float32 [1024, 1024], P(None, 'tensor')
- key_grad: float32 [1024, 1024], P(None, 'tensor')
- value_grad: float32 [1024, 1024], P(None, 'tensor')
- output_grad: float32 [1024, 1024], P('tensor')
- inner_grad: float32 [1024, 4096], P(None, 'tensor')
- outer_grad: float32 [4096, 1024], P('tensor')
- gain_entry: float32 [1024], replicated
- bias_entry: float32 [1024], replicated
- gain_merge: float32 [1024], replicated
- bias_merge: float32 [1024], replicated
- gain_inlet: float32 [1024], replicated
- bias_inlet: float32 [1024], replicated
- gain_outlet: float32 [1024], replicated
- bias_outlet: float32 [1024], replicated
Inputs may be any that keep to these rules, and one draw needn't show every extreme that they name: `lengths`: each row lists the 8 sequences of one buffer packed in order from its first row; they sum to at most 512, the rest of the buffer is padding; slots may be empty; some buffer holds a single sequence of exactly 512.
All inputs are finite; a program needn't handle non-finite values.
Results may differ from a plain program's by a relative error of at most 0.015.
The roundings to bfloat16 on the way count: a program that leaves them out, or rounds other values in their place, can miss the bound.
Values may be sent and summed in bfloat16 or wider, within the bound.
No kernel may reach another device: no remote copies, remote signals or barrier semaphores. Data moves between devices by JAX's collectives and lax.ppermute only.
A program may use at most 192 MiB of HBM per device.

v0:
```python
import math
import jax
import jax.numpy as jnp
from jax import lax
from jax.sharding import PartitionSpec as P

HEAD = 64
NEGATIVE = -1e30


def layer_norm(values, gain, bias):
    center = values - jnp.mean(values, axis=-1, keepdims=True)
    spread = jnp.mean(center * center, axis=-1, keepdims=True)
    return center * lax.rsqrt(spread + 1e-05) * gain + bias


def exact_gelu(values):
    return jax.nn.gelu(values, approximate=False)


def seq_layout(lens, rows):
    ends = jnp.cumsum(lens, dtype=jnp.int32)
    index = jnp.arange(rows, dtype=jnp.int32)
    after = index[:, None] >= ends[None, :]
    segment = jnp.sum(after.astype(jnp.int32), axis=1)
    begin = jnp.max(jnp.where(after, ends[None, :], 0), axis=1)
    return (segment, (index - begin).astype(jnp.float32))


def rotary_tables(place, width):
    half = width // 2
    rate = jnp.exp(jnp.arange(half, dtype=jnp.float32) * (-math.log(10000.0) / half))
    angle = place[:, None] * rate[None, :]
    return (jnp.cos(angle)[:, None, :], jnp.sin(angle)[:, None, :])


def rotate(values, cosine, sine):
    half = values.shape[-1] // 2
    first = values[..., :half]
    second = values[..., half:]
    return jnp.concatenate(
        [first * cosine - second * sine, first * sine + second * cosine], axis=-1
    )


def rotate_back(grads, cosine, sine):
    half = grads.shape[-1] // 2
    first = grads[..., :half]
    second = grads[..., half:]
    return jnp.concatenate(
        [first * cosine + second * sine, second * cosine - first * sine], axis=-1
    )


def contract_rows(left, right):
    return lax.dot_general(
        left, right, (((0,), (0,)), ((), ())), preferred_element_type=jnp.float32
    )


def times_transpose(left, right):
    return lax.dot_general(
        left, right, (((1,), (1,)), ((), ())), preferred_element_type=jnp.float32
    )


def masked_scores(query_block, keys, segment, begin, block):
    rows = keys.shape[0]
    scores = (
        jnp.einsum("qhd,khd->hqk", query_block, keys, preferred_element_type=jnp.float32) * 0.125
    )
    query_index = begin + jnp.arange(block, dtype=jnp.int32)
    key_index = jnp.arange(rows, dtype=jnp.int32)
    allowed = (segment[:, None] == segment[None, :]) & (key_index[None, :] <= query_index[:, None])
    return jnp.where(allowed[None], scores, NEGATIVE)


def attend_forward(query, keys, values, segment, block):
    rows = keys.shape[0]

    def one_block(number):
        begin = number * block
        scores = masked_scores(query, keys, segment, begin, block)
        peak = jnp.max(scores, axis=-1, keepdims=True)
        raised = jnp.exp(scores - peak)
        total = jnp.sum(raised, axis=-1, keepdims=True)
        probs = (raised / total).astype(jnp.bfloat16)
        attended = jnp.einsum("hqk,khd->qhd", probs, values, preferred_element_type=jnp.float32)
        return (attended, (peak + jnp.log(total))[..., 0])

    attended, logsum = lax.map(one_block, jnp.arange(rows // block, dtype=jnp.int32))
    return (attended.reshape(rows, query.shape[1], query.shape[2]), logsum)


def attend_backward(query, keys, values, mixed_grad, segment, logsum, block):
    rows = keys.shape[0]

    def one_block(carry, packed):
        keys_acc, values_acc = carry
        number, block_logsum = packed
        begin = number * block
        scores = masked_scores(query, keys, segment, begin, block)
        probs = jnp.exp(scores - block_logsum[..., None])
        prob_grad = jnp.einsum(
            "qhd,khd->hqk", mixed_grad, values, preferred_element_type=jnp.float32
        )
        offset = jnp.sum(probs * prob_grad, axis=-1, keepdims=True)
        score_grad = (probs * (prob_grad - offset)).astype(jnp.bfloat16)
        query_part = (
            jnp.einsum("hqk,khd->qhd", score_grad, keys, preferred_element_type=jnp.float32) * 0.125
        )
        keys_acc = (
            keys_acc
            + jnp.einsum("hqk,qhd->khd", score_grad, query, preferred_element_type=jnp.float32)
            * 0.125
        )
        values_acc = values_acc + jnp.einsum(
            "hqk,qhd->khd",
            probs.astype(jnp.bfloat16),
            mixed_grad,
            preferred_element_type=jnp.float32,
        )
        return ((keys_acc, values_acc), query_part)

    empty = jnp.zeros(keys.shape, jnp.float32)
    numbers = jnp.arange(rows // block, dtype=jnp.int32)
    (keys_grad, values_grad), query_grad = lax.scan(one_block, (empty, empty), (numbers, logsum))
    return (query_grad.reshape(keys.shape), keys_grad, values_grad)


def on_device(
    inputs,
    lengths,
    query_weight,
    key_weight,
    value_weight,
    output_weight,
    inner_weight,
    outer_weight,
    entry_gain,
    entry_bias,
    merge_gain,
    merge_bias,
    inlet_gain,
    inlet_bias,
    outlet_gain,
    outlet_bias,
    cotangent,
):
    groups = lax.axis_size("tensor")
    local_rows = inputs.shape[1]
    rows = local_rows * groups
    width = query_weight.shape[1]
    block = min(512, rows)
    joined = jnp.concatenate([query_weight, key_weight, value_weight], axis=1)
    inner_use, outer_use = (inner_weight, outer_weight)
    joined_acc = jnp.zeros(joined.shape, jnp.float32)
    output_acc = jnp.zeros(output_weight.shape, jnp.float32)
    inner_acc = jnp.zeros(inner_use.shape, jnp.float32)
    outer_acc = jnp.zeros(outer_use.shape, jnp.float32)
    norm_acc = [jnp.zeros(entry_gain.shape, jnp.float32) for index in range(8)]
    result_list = []
    grad_list = []
    for micro in range(inputs.shape[0]):
        segment, place = seq_layout(lengths[micro, 0], rows)
        cosine, sine = rotary_tables(place, HEAD)
        resid = inputs[micro].astype(jnp.float32)
        normed, entry_pull = jax.vjp(layer_norm, resid, entry_gain, entry_bias)
        gathered = lax.all_gather(normed.astype(jnp.bfloat16), "tensor", axis=0, tiled=True)
        projected = jnp.dot(gathered, joined, preferred_element_type=jnp.float32)
        query = rotate(
            projected[:, :width].reshape(rows, width // HEAD, HEAD), cosine, sine
        ).astype(jnp.bfloat16)
        keys = rotate(
            projected[:, width : 2 * width].reshape(rows, width // HEAD, HEAD), cosine, sine
        ).astype(jnp.bfloat16)
        values = projected[:, 2 * width :].reshape(rows, width // HEAD, HEAD).astype(jnp.bfloat16)
        attended, logsum = attend_forward(query, keys, values, segment, block)
        mixed = attended.reshape(rows, width).astype(jnp.bfloat16)
        branch = lax.psum_scatter(
            jnp.dot(mixed, output_weight, preferred_element_type=jnp.float32),
            "tensor",
            scatter_dimension=0,
            tiled=True,
        )
        merged, merge_pull = jax.vjp(layer_norm, branch, merge_gain, merge_bias)
        hidden = resid + merged
        inlet, inlet_pull = jax.vjp(layer_norm, hidden, inlet_gain, inlet_bias)
        inlet_low = inlet.astype(jnp.bfloat16)
        feed = lax.all_gather(inlet_low, "tensor", axis=0, tiled=True)
        pre_act = jnp.dot(feed, inner_use, preferred_element_type=jnp.float32)
        activated, gelu_pull = jax.vjp(exact_gelu, pre_act)
        act_low = activated.astype(jnp.bfloat16)
        second = lax.psum_scatter(
            jnp.dot(act_low, outer_use, preferred_element_type=jnp.float32),
            "tensor",
            scatter_dimension=0,
            tiled=True,
        )
        finished, outlet_pull = jax.vjp(layer_norm, second, outlet_gain, outlet_bias)
        result_list.append((hidden + finished).astype(jnp.bfloat16))
        upstream = cotangent[micro].astype(jnp.float32)
        second_grad, outlet_gain_part, outlet_bias_part = outlet_pull(upstream)
        second_low = second_grad.astype(jnp.bfloat16)
        back_feed = lax.all_gather(second_low, "tensor", axis=0, tiled=True)
        outer_term = contract_rows(act_low, back_feed)
        act_grad = times_transpose(back_feed, outer_use)
        (pre_grad,) = gelu_pull(act_grad)
        pre_low = pre_grad.astype(jnp.bfloat16)
        inner_term = contract_rows(feed, pre_low)
        inlet_grad = lax.psum_scatter(
            times_transpose(pre_low, inner_use), "tensor", scatter_dimension=0, tiled=True
        )
        hidden_part, inlet_gain_part, inlet_bias_part = inlet_pull(inlet_grad)
        hidden_grad = upstream + hidden_part
        branch_grad, merge_gain_part, merge_bias_part = merge_pull(hidden_grad)
        back_mix = lax.all_gather(branch_grad.astype(jnp.bfloat16), "tensor", axis=0, tiled=True)
        output_term = contract_rows(mixed, back_mix)
        mixed_grad = (
            times_transpose(back_mix, output_weight)
            .astype(jnp.bfloat16)
            .reshape(rows, width // HEAD, HEAD)
        )
        query_part, keys_part, values_part = attend_backward(
            query, keys, values, mixed_grad, segment, logsum, block
        )
        projected_grad = jnp.concatenate(
            [
                rotate_back(query_part, cosine, sine).reshape(rows, width),
                rotate_back(keys_part, cosine, sine).reshape(rows, width),
                values_part.reshape(rows, width),
            ],
            axis=1,
        ).astype(jnp.bfloat16)
        joined_term = contract_rows(gathered, projected_grad)
        normed_grad = lax.psum_scatter(
            times_transpose(projected_grad, joined).astype(jnp.bfloat16),
            "tensor",
            scatter_dimension=0,
            tiled=True,
        ).astype(jnp.float32)
        resid_part, entry_gain_part, entry_bias_part = entry_pull(normed_grad)
        grad_list.append((hidden_grad + resid_part).astype(jnp.bfloat16))
        parts = [
            entry_gain_part,
            entry_bias_part,
            merge_gain_part,
            merge_bias_part,
            inlet_gain_part,
            inlet_bias_part,
            outlet_gain_part,
            outlet_bias_part,
        ]
        norm_acc = [total + piece for total, piece in zip(norm_acc, parts)]
        joined_acc = joined_acc + joined_term
        output_acc = output_acc + output_term
        inner_acc = inner_acc + inner_term
        outer_acc = outer_acc + outer_term
    joined_acc, output_acc, inner_acc, outer_acc = lax.psum(
        (joined_acc, output_acc, inner_acc, outer_acc), "dp"
    )
    norm_sums = lax.psum(
        (
            norm_acc[0],
            norm_acc[1],
            norm_acc[2],
            norm_acc[3],
            norm_acc[4],
            norm_acc[5],
            norm_acc[6],
            norm_acc[7],
        ),
        ("dp", "tensor"),
    )
    return (
        jnp.stack(result_list),
        jnp.stack(grad_list),
        joined_acc[:, :width],
        joined_acc[:, width : 2 * width],
        joined_acc[:, 2 * width :],
        output_acc,
        inner_acc,
        outer_acc,
        norm_sums[0],
        norm_sums[1],
        norm_sums[2],
        norm_sums[3],
        norm_sums[4],
        norm_sums[5],
        norm_sums[6],
        norm_sums[7],
    )


def solution(mesh):
    placed = (
        P(None, ("dp", "tensor"), None),
        P(None, "dp", None),
        P(None, "tensor"),
        P(None, "tensor"),
        P(None, "tensor"),
        P("tensor", None),
        P(None, "tensor"),
        P("tensor", None),
        P(),
        P(),
        P(),
        P(),
        P(),
        P(),
        P(),
        P(),
        P(None, ("dp", "tensor"), None),
    )
    return jax.shard_map(
        on_device,
        mesh=mesh,
        in_specs=placed,
        out_specs=(
            P(None, ("dp", "tensor"), None),
            P(None, ("dp", "tensor"), None),
            P(None, "tensor"),
            P(None, "tensor"),
            P(None, "tensor"),
            P("tensor", None),
            P(None, "tensor"),
            P("tensor", None),
            P(),
            P(),
            P(),
            P(),
            P(),
            P(),
            P(),
            P(),
        ),
        check_vma=False,
    )
```

profile of v0, /device:TPU:0, one launch (start us, length us, event | category | flops | bytes accessed | tf_op | source)
XLA Modules:
  0.0 979.6 jit_solution(8197130521890826717)
XLA Ops:
  21.8 3.9 all-gather.13.cloned.1.call-done
  25.8 4.0 fusion.125
  36.1 2.7 fusion.121
  47.3 4.0 fusion.122
  70.1 8.1 reduce-scatter.9.cloned.1.call-done
  86.6 9.5 all-gather.15.cloned.1.call-done
  96.1 15.0 %multiply_convert_fusion.2 = (bf16[512,2048]{1,0:T(8,128)(2,1)S(1)}, f32[512,2048]{1,0:T(8,128)}, f32[512,2048]{1,0:T(8,128)}) fusion(bf16[512,1024]{1,0:T(8,128)(2,1)} %all-gather.15.cloned.1.call-done, bf16[1024,2048]{1,0:T(8,128)(2,1)} %param.23), kind=kOutput, calls=%fused_computation.27 | convolution fusion | flops 2215641088 | bytes 15728640 | tf_op jit(solution)/shard_map/dot_general | solution.py:191
  112.5 3.6 fusion.127
  116.6 14.9 %multiply_convert_fusion.3 = (bf16[512,2048]{1,0:T(8,128)(2,1)S(1)}, f32[512,2048]{1,0:T(8,128)}, f32[512,2048]{1,0:T(8,128)}) fusion(bf16[512,1024]{1,0:T(8,128)(2,1)} %all-gather.11.cloned.1.call-done, bf16[1024,2048]{1,0:T(8,128)(2,1)} %param.23), kind=kOutput, calls=%fused_computation.40 | convolution fusion | flops 2215641088 | bytes 15728640 | tf_op jit(solution)/shard_map/dot_general | solution.py:191
  132.8 3.6 fusion.124
  139.5 7.9 reduce-scatter.11.cloned.1.call-done
  150.5 2.7 fusion.72
  158.7 7.9 all-gather.21.cloned.1.call-done
  166.6 8.5 add_convert_fusion
  176.5 3.7 fusion.129
  180.3 8.5 add_convert_fusion.1
  190.2 3.7 fusion.128
  194.2 7.5 fusion.132
  201.7 4.4 reduce-scatter.17.cloned.1.call-done
  214.1 9.5 convolution_add_fusion.1
  223.7 5.7 fusion.131
  232.9 5.4 multiply_reduce_fusion
  246.5 2.8 convolution_convert_fusion
  251.6 5.4 multiply_reduce_fusion.1
  265.3 2.8 convolution_convert_fusion.1
  268.4 9.9 %convolution_add_fusion.2 = f32[1024,2048]{1,0:T(8,128)} fusion(f32[1024,2048]{1,0:T(8,128)} %fusion.131, bf16[512,1024]{1,0:T(8,128)(2,1)S(1)} %copy-done.22, bf16[512,2048]{1,0:T(8,128)(2,1)} %copy-done.23), kind=kOutput, calls=%fused_computation.58 | convolution fusion | flops 2149580800 | bytes 19922944 | tf_op jit(solution)/shard_map/dot_general | solution.py:56
  283.6 4.6 convolution_add_fusion
  296.6 45.4 %all-reduce = (f32[1024]{0:T(1024)}, f32[1024]{0:T(1024)}, f32[1024]{0:T(1024)}, f32[1024]{0:T(1024)}, f32[1024]{0:T(1024)}, /*index=5*/f32[1024]{0:T(1024)}, f32[1024]{0:T(1024)}, f32[1024]{0:T(1024)}) all-reduce(f32[1024]{0:T(1024)S(1)} %add.355, f32[1024]{0:T(1024)S(1)} %add.356, ...), channel_id=1, replica_groups=mesh['dp'=16,'tensor'=2] {'dp','tensor'}, use_global_device_ids=true, to_apply=%region_58.59 | all-reduce | flops 8192 | bytes 65536 | tf_op jit(solution)/shard_map/psum | solution.py:262
  345.6 609.3 %all-reduce.4.cloned.1.call-done = (f32[1024,1536]{1,0:T(8,128)}, f32[512,1024]{1,0:T(8,128)}, f32[1024,2048]{1,0:T(8,128)}, f32[2048,1024]{1,0:T(8,128)}) async-done(((f32[1024,1536]{1,0:T(8,128)}, f32[512,1024]{1,0:T(8,128)}, f32[1024,2048]{1,0:T(8,128)}, f32[2048,1024]{1,0:T(8,128)}), (f32[1024,1536]{1,0:T(8,128)}, f32[512,1024]{1,0:T(8,128)}, f32[1024,2048]{1,0:T(8,128)}, ...) | async-done | bytes 25165840 | tf_op jit(solution)/shard_map/psum | solution.py:259
  954.9 6.3 fusion.117
  963.8 4.3 copy.94
  969.5 3.4 copy.95
  (399 shorter events, 124.5 us)
Async XLA Ops:
  7.2 37.5 %copy-start = (bf16[512,1024]{1,0:T(8,128)(2,1)S(1)}, bf16[512,1024]{1,0:T(8,128)(2,1)}, u32[]{:S(2)}) copy-start(bf16[512,1024]{1,0:T(8,128)(2,1)} %param.22) | copy-start | bytes 3145732
  7.2 18.5 %all-gather.13.cloned.1.call-start = ((), (), s32[]{:S(2)}) async-start(), calls=%async_computation.12 | async-start | bytes 1572864 | tf_op jit(solution)/shard_map/all_gather | solution.py:169
  13.8 33.5 %all-gather.9.cloned.1.call-start = ((), (), s32[]{:S(2)}) async-start(), calls=%async_computation.8 | async-start | bytes 1572864 | tf_op jit(solution)/shard_map/all_gather | solution.py:169
  14.5 52.7 %reduce-scatter.13.cloned.1.call-start = ((), (), s32[]{:S(2)}) async-start(), calls=%async_computation.13 | async-start | bytes 3145728 | tf_op jit(solution)/shard_map/reduce_scatter | solution.py:180
  21.8 13.9 %copy-start.62 = (f32[512,32]{0,1:T(8,128)}, f32[512,32]{0,1:T(8,128)S(1)}, u32[]{:S(2)}) copy-start(f32[512,32]{0,1:T(8,128)S(1)} %get-tuple-element.251) | copy-start | bytes 196612
  21.8 13.9 %copy-start.64 = (f32[512,32]{0,1:T(8,128)}, f32[512,32]{0,1:T(8,128)S(1)}, u32[]{:S(2)}) copy-start(f32[512,32]{0,1:T(8,128)S(1)} %get-tuple-element.252) | copy-start | bytes 196612
  21.8 35.5 %copy-start.58 = (f32[512,32]{0,1:T(8,128)}, f32[512,32]{0,1:T(8,128)S(1)}, u32[]{:S(2)}) copy-start(f32[512,32]{0,1:T(8,128)S(1)} %get-tuple-element.245) | copy-start | bytes 196612
  21.8 35.5 %copy-start.60 = (f32[512,32]{0,1:T(8,128)}, f32[512,32]{0,1:T(8,128)S(1)}, u32[]{:S(2)}) copy-start(f32[512,32]{0,1:T(8,128)S(1)} %get-tuple-element.246) | copy-start | bytes 196612
  46.8 31.4 %reduce-scatter.9.cloned.1.call-start = ((), (), s32[]{:S(2)}) async-start(), calls=%async_computation.9 | async-start | bytes 3145728 | tf_op jit(solution)/shard_map/reduce_scatter | solution.py:180
  65.1 16.0 %copy-start.3 = (bf16[2,256,1024]{2,1,0:T(8,128)(2,1)S(1)}, bf16[2,256,1024]{2,1,0:T(8,128)(2,1)}, u32[]{:S(2)}) copy-start(bf16[2,256,1024]{2,1,0:T(8,128)(2,1)} %param.17) | copy-start | bytes 3145732
  65.1 16.0 %copy-start.82 = (f32[1024]{0:T(1024)S(1)}, f32[1024]{0:T(1024)}, u32[]{:S(2)}) copy-start(f32[1024]{0:T(1024)} %param.27) | copy-start | bytes 12292
  65.1 16.0 %copy-start.95 = (f32[1024]{0:T(1024)S(1)}, f32[1024]{0:T(1024)}, u32[]{:S(2)}) copy-start(f32[1024]{0:T(1024)} %param.28) | copy-start | bytes 12292
  67.2 28.9 %all-gather.15.cloned.1.call-start = ((), (), s32[]{:S(2)}) async-start(), calls=%async_computation.14 | async-start | bytes 1572864 | tf_op jit(solution)/shard_map/all_gather | solution.py:190
  85.7 30.9 %all-gather.11.cloned.1.call-start = ((), (), s32[]{:S(2)}) async-start(), calls=%async_computation.10 | async-start | bytes 1572864 | tf_op jit(solution)/shard_map/all_gather | solution.py:190
  86.3 50.3 %reduce-scatter.15.cloned.1.call-start = ((), (), s32[]{:S(2)}) async-start(), calls=%async_computation.15 | async-start | bytes 3145728 | tf_op jit(solution)/shard_map/reduce_scatter | solution.py:194
  96.1 16.3 %copy-start.97 = (bf16[2048,1024]{1,0:T(8,128)(2,1)S(1)}, bf16[2048,1024]{1,0:T(8,128)(2,1)}, u32[]{:S(2)}) copy-start(bf16[2048,1024]{1,0:T(8,128)(2,1)} %param.24) | copy-start | bytes 12582916
  116.1 31.3 %reduce-scatter.11.cloned.1.call-start = ((), (), s32[]{:S(2)}) async-start(), calls=%async_computation.11 | async-start | bytes 3145728 | tf_op jit(solution)/shard_map/reduce_scatter | solution.py:194
  116.6 16.2 %copy-start.98 = (bf16[2048,1024]{1,0:T(8,128)(2,1)S(1)}, bf16[2048,1024]{1,0:T(8,128)(2,1)}, u32[]{:S(2)}) copy-start(bf16[2048,1024]{1,0:T(8,128)(2,1)} %param.24) | copy-start | bytes 12582916
  136.5 14.0 %copy-start.84 = (f32[1024]{0:T(1024)S(1)}, f32[1024]{0:T(1024)}, u32[]{:S(2)}) copy-start(f32[1024]{0:T(1024)} %param.31) | copy-start | bytes 12292
  136.5 16.7 %copy-start.6 = (f32[256,1024]{1,0:T(8,128)S(1)}, f32[256,1024]{1,0:T(8,128)}, u32[]{:S(2)}) copy-start(f32[256,1024]{1,0:T(8,128)} %copy-done.5) | copy-start | bytes 3145732
  136.5 16.7 %copy-start.94 = (f32[1024]{0:T(1024)S(1)}, f32[1024]{0:T(1024)}, u32[]{:S(2)}) copy-start(f32[1024]{0:T(1024)} %param.32) | copy-start | bytes 12292
  136.5 30.1 %all-gather.21.cloned.1.call-start = ((), (), s32[]{:S(2)}) async-start(), calls=%async_computation.20 | async-start | bytes 1572864 | tf_op jit(solution)/shard_map/all_gather | solution.py:205
  156.3 24.0 %all-gather.17.cloned.1.call-start = ((), (), s32[]{:S(2)}) async-start(), calls=%async_computation.16 | async-start | bytes 1572864 | tf_op jit(solution)/shard_map/all_gather | solution.py:205
  158.5 43.2 %reduce-scatter.21.cloned.1.call-start = ((), (), s32[]{:S(2)}) async-start(), calls=%async_computation.21 | async-start | bytes 3145728 | tf_op jit(solution)/shard_map/reduce_scatter | solution.py:211
  180.2 25.8 %reduce-scatter.17.cloned.1.call-start = ((), (), s32[]{:S(2)}) async-start(), calls=%async_computation.17 | async-start | bytes 3145728 | tf_op jit(solution)/shard_map/reduce_scatter | solution.py:211
  193.9 37.0 %all-gather.23.cloned.1.call-start = ((), (), s32[]{:S(2)}) async-start(), calls=%async_computation.22 | async-start | bytes 1572864 | tf_op jit(solution)/shard_map/all_gather | solution.py:217
  214.0 35.5 %all-gather.19.cloned.1.call-start = ((), (), s32[]{:S(2)}) async-start(), calls=%async_computation.18 | async-start | bytes 1572864 | tf_op jit(solution)/shard_map/all_gather | solution.py:217
  230.4 61.7 %reduce-scatter.23.cloned.1.call-start = ((), (), s32[]{:S(2)}) async-start(), calls=%async_computation.23 | async-start | bytes 1572864 | tf_op jit(solution)/shard_map/reduce_scatter | solution.py:236
  249.3 42.8 %reduce-scatter.19.cloned.1.call-start = ((), (), s32[]{:S(2)}) async-start(), calls=%async_computation.19 | async-start | bytes 1572864 | tf_op jit(solution)/shard_map/reduce_scatter | solution.py:236
  268.2 686.7 %all-reduce.4.cloned.1.call-start = ((), (), s32[]{:S(2)}) async-start(), calls=%async_computation.24 | async-start | bytes 50331648 | tf_op jit(solution)/shard_map/psum | solution.py:259
  268.4 10.7 %copy-start.36 = (bf16[8,64,512]{2,1,0:T(8,128)(2,1)S(1)}, bf16[8,64,512]{2,1,0:T(8,128)(2,1)}, u32[]{:S(2)}) copy-start(bf16[8,64,512]{2,1,0:T(8,128)(2,1)} %copy-done.35) | copy-start | bytes 1572868
  289.6 52.5 %copy-start.15 = (f32[256,1024]{1,0:T(8,128)S(1)}, f32[256,1024]{1,0:T(8,128)}, u32[]{:S(2)}) copy-start(f32[256,1024]{1,0:T(8,128)} %copy-done.14) | copy-start | bytes 3145732
  (99 other events, 349.0 us)
Sparse Core Ops, SparseCore 0:
  13.9 11.8 all-gather.12
  27.9 10.1 all-gather.8
  46.9 10.6 reduce-scatter.12
  67.3 10.8 reduce-scatter.8
  85.9 10.2 all-gather.14
  98.1 10.1 all-gather.10
  116.2 10.7 reduce-scatter.14
  136.6 10.7 reduce-scatter.10
  156.4 10.2 all-gather.20
  168.6 10.1 all-gather.16
  181.7 10.7 reduce-scatter.20
  195.2 10.7 reduce-scatter.16
  214.2 10.2 all-gather.22
  230.5 10.2 all-gather.18
  249.4 9.7 reduce-scatter.22
  268.3 9.7 reduce-scatter.18
  288.4 666.4 all-reduce.3
where the time goes:
time: 988 us; the launch traced here: 980 us
  waiting for transfers between devices  653 us (66%)
  matrix products  151 us (15%)
  other arithmetic  59.3 us (6%)
  local copies, waits for them, and re-layouts  53.1 us (5%)
  blocking collectives  45.4 us (5%)
  between operations  15.9 us (2%)
    psum x1, waiting for transfers between devices, on_device(): lax.psum((joined_acc, output_acc, inner_acc, outer_acc), 'dp')  609 us
    psum x1, blocking collectives, on_device(): lax.psum((norm_acc[0], norm_acc[1], norm_acc[2], norm_acc[3], norm_acc[4]...  45.4 us
    dot_general x8, matrix products, contract_rows(): lax.dot_general(left, right, (((0,), (0,)), ((), ())), preferred_element_...  41.9 us
    dot_general x8, matrix products, times_transpose(): lax.dot_general(left, right, (((1,), (1,)), ((), ())), preferred_element_...  34 us
    unnamed x233, local copies, waits for them, and re-layouts  32.4 us
    dot_general x2, matrix products, on_device(): pre_act = jnp.dot(feed, inner_use, preferred_element_type=jnp.float32)  29.8 us
  transfers between devices with their start and end apart: 17, of which 7 were waited for; matrix products, arithmetic and copies ran while one was open for 20% of the time, Pallas kernels for 0%

commit v1 on v0

--- a/solution.py
+++ b/solution.py
@@ -260,17 +260,20 @@
         (joined_acc, output_acc, inner_acc, outer_acc), "dp"
     )
     norm_sums = lax.psum(
-        (
-            norm_acc[0],
-            norm_acc[1],
-            norm_acc[2],
-            norm_acc[3],
-            norm_acc[4],
-            norm_acc[5],
-            norm_acc[6],
-            norm_acc[7],
+        lax.psum(
+            (
+                norm_acc[0],
+                norm_acc[1],
+                norm_acc[2],
+                norm_acc[3],
+                norm_acc[4],
+                norm_acc[5],
+                norm_acc[6],
+                norm_acc[7],
+            ),
+            "tensor",
         ),
-        ("dp", "tensor"),
+        "dp",
     )
     return (
         jnp.stack(result_list),

time: 988 us -> 988 us (level)
  waiting for transfers between devices: 653 us -> 612 us
  blocking collectives: 45.4 us -> 85.6 us
    psum x0 -> x1, blocking collectives: none -> 82.2 us  [on_device(): lax.psum(lax.psum((norm_acc[0], norm_acc[1], norm_acc[2], norm_acc[3], no...]
    psum x1, blocking collectives: 45.4 us -> 3.46 us  [on_device(): lax.psum((norm_acc[0], norm_acc[1], norm_acc[2], norm_acc[3], norm_acc[4]...]
    psum x1, waiting for transfers between devices: 609 us -> 569 us  [on_device(): lax.psum((joined_acc, output_acc, inner_acc, outer_acc), 'dp')]
where the time goes in v1:
time: 988 us; the launch traced here: 979 us
  waiting for transfers between devices  612 us (62%)
  matrix products  150 us (15%)
  blocking collectives  85.6 us (9%)
  other arithmetic  59.4 us (6%)
  local copies, waits for them, and re-layouts  53.1 us (5%)
  between operations  15.9 us (2%)
    psum x1, waiting for transfers between devices, on_device(): lax.psum((joined_acc, output_acc, inner_acc, outer_acc), 'dp')  569 us
    psum x1, blocking collectives, on_device(): lax.psum(lax.psum((norm_acc[0], norm_acc[1], norm_acc[2], norm_acc[3], no...  82.2 us
    dot_general x8, matrix products, contract_rows(): lax.dot_general(left, right, (((0,), (0,)), ((), ())), preferred_element_...  41.9 us
    dot_general x8, matrix products, times_transpose(): lax.dot_general(left, right, (((1,), (1,)), ((), ())), preferred_element_...  34 us
    unnamed x233, local copies, waits for them, and re-layouts  32.3 us
    dot_general x2, matrix products, on_device(): pre_act = jnp.dot(feed, inner_use, preferred_element_type=jnp.float32)  29.7 us
  transfers between devices with their start and end apart: 17, of which 7 were waited for; matrix products, arithmetic and copies ran while one was open for 20% of the time, Pallas kernels for 0%

profile of v1, /device:TPU:0, one launch (start us, length us, event | category | flops | bytes accessed | tf_op | source)
XLA Modules:
  0.0 979.4 jit_solution(17474209392059507621)
XLA Ops:
  21.8 3.9 all-gather.13.cloned.1.call-done
  25.8 4.0 fusion.125
  36.1 2.7 fusion.121
  47.2 4.0 fusion.122
  70.1 8.1 reduce-scatter.9.cloned.1.call-done
  86.6 9.5 all-gather.15.cloned.1.call-done
  96.1 14.9 %multiply_convert_fusion.2 = (bf16[512,2048]{1,0:T(8,128)(2,1)S(1)}, f32[512,2048]{1,0:T(8,128)}, f32[512,2048]{1,0:T(8,128)}) fusion(bf16[512,1024]{1,0:T(8,128)(2,1)} %all-gather.15.cloned.1.call-done, bf16[1024,2048]{1,0:T(8,128)(2,1)} %param.23), kind=kOutput, calls=%fused_computation.27 | convolution fusion | flops 2215641088 | bytes 15728640 | tf_op jit(solution)/shard_map/dot_general | solution.py:191
  112.4 3.6 fusion.127
  116.5 14.8 %multiply_convert_fusion.3 = (bf16[512,2048]{1,0:T(8,128)(2,1)S(1)}, f32[512,2048]{1,0:T(8,128)}, f32[512,2048]{1,0:T(8,128)}) fusion(bf16[512,1024]{1,0:T(8,128)(2,1)} %all-gather.11.cloned.1.call-done, bf16[1024,2048]{1,0:T(8,128)(2,1)} %param.23), kind=kOutput, calls=%fused_computation.40 | convolution fusion | flops 2215641088 | bytes 15728640 | tf_op jit(solution)/shard_map/dot_general | solution.py:191
  132.7 3.6 fusion.124
  139.4 7.9 reduce-scatter.11.cloned.1.call-done
  158.6 7.9 all-gather.21.cloned.1.call-done
  166.5 8.5 add_convert_fusion
  176.3 3.7 fusion.129
  180.1 8.5 add_convert_fusion.1
  190.0 3.7 fusion.128
  194.0 7.5 fusion.132
  201.5 4.4 reduce-scatter.17.cloned.1.call-done
  214.0 9.5 convolution_add_fusion.1
  223.5 5.7 fusion.131
  232.7 5.4 multiply_reduce_fusion
  246.3 2.8 convolution_convert_fusion
  251.4 5.4 multiply_reduce_fusion.1
  265.1 2.8 convolution_convert_fusion.1
  268.3 9.9 %convolution_add_fusion.2 = f32[1024,2048]{1,0:T(8,128)} fusion(f32[1024,2048]{1,0:T(8,128)} %fusion.131, bf16[512,1024]{1,0:T(8,128)(2,1)S(1)} %copy-done.22, bf16[512,2048]{1,0:T(8,128)(2,1)} %copy-done.23), kind=kOutput, calls=%fused_computation.58 | convolution fusion | flops 2149580800 | bytes 19922944 | tf_op jit(solution)/shard_map/dot_general | solution.py:56
  283.4 4.6 convolution_add_fusion
  296.4 3.5 all-reduce.2
  299.9 82.2 %all-reduce = (f32[1024]{0:T(1024)}, f32[1024]{0:T(1024)}, f32[1024]{0:T(1024)}, f32[1024]{0:T(1024)}, f32[1024]{0:T(1024)}, /*index=5*/f32[1024]{0:T(1024)}, f32[1024]{0:T(1024)}, f32[1024]{0:T(1024)}) all-reduce(f32[1024]{0:T(1024)S(1)} %get-tuple-element.168, ...), channel_id=1, replica_groups=mesh['dp'=16,'tensor'=2] {'dp'}, use_global_device_ids=true, to_apply=%region_59.60 | all-reduce | flops 8192 | bytes 65536 | tf_op jit(solution)/shard_map/psum | solution.py:262
  385.7 569.0 %all-reduce.5.cloned.1.call-done = (f32[1024,1536]{1,0:T(8,128)}, f32[512,1024]{1,0:T(8,128)}, f32[1024,2048]{1,0:T(8,128)}, f32[2048,1024]{1,0:T(8,128)}) async-done(((f32[1024,1536]{1,0:T(8,128)}, f32[512,1024]{1,0:T(8,128)}, f32[1024,2048]{1,0:T(8,128)}, f32[2048,1024]{1,0:T(8,128)}), (f32[1024,1536]{1,0:T(8,128)}, f32[512,1024]{1,0:T(8,128)}, f32[1024,2048]{1,0:T(8,128)}, ...) | async-done | bytes 25165840 | tf_op jit(solution)/shard_map/psum | solution.py:259
  954.7 6.3 fusion.117
  963.6 4.3 copy.94
  969.3 3.4 copy.95
  (400 shorter events, 127.3 us)
Async XLA Ops:
  7.2 37.5 %copy-start = (bf16[512,1024]{1,0:T(8,128)(2,1)S(1)}, bf16[512,1024]{1,0:T(8,128)(2,1)}, u32[]{:S(2)}) copy-start(bf16[512,1024]{1,0:T(8,128)(2,1)} %param.22) | copy-start | bytes 3145732
  7.2 18.5 %all-gather.13.cloned.1.call-start = ((), (), s32[]{:S(2)}) async-start(), calls=%async_computation.12 | async-start | bytes 1572864 | tf_op jit(solution)/shard_map/all_gather | solution.py:169
  13.8 33.5 %all-gather.9.cloned.1.call-start = ((), (), s32[]{:S(2)}) async-start(), calls=%async_computation.8 | async-start | bytes 1572864 | tf_op jit(solution)/shard_map/all_gather | solution.py:169
  14.5 52.7 %reduce-scatter.13.cloned.1.call-start = ((), (), s32[]{:S(2)}) async-start(), calls=%async_computation.13 | async-start | bytes 3145728 | tf_op jit(solution)/shard_map/reduce_scatter | solution.py:180
  21.8 13.9 %copy-start.62 = (f32[512,32]{0,1:T(8,128)}, f32[512,32]{0,1:T(8,128)S(1)}, u32[]{:S(2)}) copy-start(f32[512,32]{0,1:T(8,128)S(1)} %get-tuple-element.259) | copy-start | bytes 196612
  21.8 13.9 %copy-start.64 = (f32[512,32]{0,1:T(8,128)}, f32[512,32]{0,1:T(8,128)S(1)}, u32[]{:S(2)}) copy-start(f32[512,32]{0,1:T(8,128)S(1)} %get-tuple-element.260) | copy-start | bytes 196612
  21.8 35.5 %copy-start.58 = (f32[512,32]{0,1:T(8,128)}, f32[512,32]{0,1:T(8,128)S(1)}, u32[]{:S(2)}) copy-start(f32[512,32]{0,1:T(8,128)S(1)} %get-tuple-element.253) | copy-start | bytes 196612
  21.8 35.5 %copy-start.60 = (f32[512,32]{0,1:T(8,128)}, f32[512,32]{0,1:T(8,128)S(1)}, u32[]{:S(2)}) copy-start(f32[512,32]{0,1:T(8,128)S(1)} %get-tuple-element.254) | copy-start | bytes 196612
  46.8 31.4 %reduce-scatter.9.cloned.1.call-start = ((), (), s32[]{:S(2)}) async-start(), calls=%async_computation.9 | async-start | bytes 3145728 | tf_op jit(solution)/shard_map/reduce_scatter | solution.py:180
  65.1 16.0 %copy-start.3 = (bf16[2,256,1024]{2,1,0:T(8,128)(2,1)S(1)}, bf16[2,256,1024]{2,1,0:T(8,128)(2,1)}, u32[]{:S(2)}) copy-start(bf16[2,256,1024]{2,1,0:T(8,128)(2,1)} %param.17) | copy-start | bytes 3145732
  65.1 16.0 %copy-start.82 = (f32[1024]{0:T(1024)S(1)}, f32[1024]{0:T(1024)}, u32[]{:S(2)}) copy-start(f32[1024]{0:T(1024)} %param.27) | copy-start | bytes 12292
  65.1 16.0 %copy-start.95 = (f32[1024]{0:T(1024)S(1)}, f32[1024]{0:T(1024)}, u32[]{:S(2)}) copy-start(f32[1024]{0:T(1024)} %param.28) | copy-start | bytes 12292
  67.2 28.9 %all-gather.15.cloned.1.call-start = ((), (), s32[]{:S(2)}) async-start(), calls=%async_computation.14 | async-start | bytes 1572864 | tf_op jit(solution)/shard_map/all_gather | solution.py:190
  85.8 30.8 %all-gather.11.cloned.1.call-start = ((), (), s32[]{:S(2)}) async-start(), calls=%async_computation.10 | async-start | bytes 1572864 | tf_op jit(solution)/shard_map/all_gather | solution.py:190
  86.3 50.1 %reduce-scatter.15.cloned.1.call-start = ((), (), s32[]{:S(2)}) async-start(), calls=%async_computation.15 | async-start | bytes 3145728 | tf_op jit(solution)/shard_map/reduce_scatter | solution.py:194
  96.1 16.2 %copy-start.97 = (bf16[2048,1024]{1,0:T(8,128)(2,1)S(1)}, bf16[2048,1024]{1,0:T(8,128)(2,1)}, u32[]{:S(2)}) copy-start(bf16[2048,1024]{1,0:T(8,128)(2,1)} %param.24) | copy-start | bytes 12582916
  116.0 31.2 %reduce-scatter.11.cloned.1.call-start = ((), (), s32[]{:S(2)}) async-start(), calls=%async_computation.11 | async-start | bytes 3145728 | tf_op jit(solution)/shard_map/reduce_scatter | solution.py:194
  116.5 16.2 %copy-start.98 = (bf16[2048,1024]{1,0:T(8,128)(2,1)S(1)}, bf16[2048,1024]{1,0:T(8,128)(2,1)}, u32[]{:S(2)}) copy-start(bf16[2048,1024]{1,0:T(8,128)(2,1)} %param.24) | copy-start | bytes 12582916
  136.3 14.0 %copy-start.84 = (f32[1024]{0:T(1024)S(1)}, f32[1024]{0:T(1024)}, u32[]{:S(2)}) copy-start(f32[1024]{0:T(1024)} %param.31) | copy-start | bytes 12292
  136.3 16.7 %copy-start.6 = (f32[256,1024]{1,0:T(8,128)S(1)}, f32[256,1024]{1,0:T(8,128)}, u32[]{:S(2)}) copy-start(f32[256,1024]{1,0:T(8,128)} %copy-done.5) | copy-start | bytes 3145732
  136.4 16.7 %copy-start.94 = (f32[1024]{0:T(1024)S(1)}, f32[1024]{0:T(1024)}, u32[]{:S(2)}) copy-start(f32[1024]{0:T(1024)} %param.32) | copy-start | bytes 12292
  136.4 30.1 %all-gather.21.cloned.1.call-start = ((), (), s32[]{:S(2)}) async-start(), calls=%async_computation.20 | async-start | bytes 1572864 | tf_op jit(solution)/shard_map/all_gather | solution.py:205
  156.1 24.0 %all-gather.17.cloned.1.call-start = ((), (), s32[]{:S(2)}) async-start(), calls=%async_computation.16 | async-start | bytes 1572864 | tf_op jit(solution)/shard_map/all_gather | solution.py:205
  158.3 43.2 %reduce-scatter.21.cloned.1.call-start = ((), (), s32[]{:S(2)}) async-start(), calls=%async_computation.21 | async-start | bytes 3145728 | tf_op jit(solution)/shard_map/reduce_scatter | solution.py:211
  180.1 25.8 %reduce-scatter.17.cloned.1.call-start = ((), (), s32[]{:S(2)}) async-start(), calls=%async_computation.17 | async-start | bytes 3145728 | tf_op jit(solution)/shard_map/reduce_scatter | solution.py:211
  193.7 36.9 %all-gather.23.cloned.1.call-start = ((), (), s32[]{:S(2)}) async-start(), calls=%async_computation.22 | async-start | bytes 1572864 | tf_op jit(solution)/shard_map/all_gather | solution.py:217
  213.9 35.5 %all-gather.19.cloned.1.call-start = ((), (), s32[]{:S(2)}) async-start(), calls=%async_computation.18 | async-start | bytes 1572864 | tf_op jit(solution)/shard_map/all_gather | solution.py:217
  230.2 61.7 %reduce-scatter.23.cloned.1.call-start = ((), (), s32[]{:S(2)}) async-start(), calls=%async_computation.23 | async-start | bytes 1572864 | tf_op jit(solution)/shard_map/reduce_scatter | solution.py:236
  249.1 42.8 %reduce-scatter.19.cloned.1.call-start = ((), (), s32[]{:S(2)}) async-start(), calls=%async_computation.19 | async-start | bytes 1572864 | tf_op jit(solution)/shard_map/reduce_scatter | solution.py:236
  268.0 686.7 %all-reduce.5.cloned.1.call-start = ((), (), s32[]{:S(2)}) async-start(), calls=%async_computation.24 | async-start | bytes 50331648 | tf_op jit(solution)/shard_map/psum | solution.py:259
  268.3 10.7 %copy-start.36 = (bf16[8,64,512]{2,1,0:T(8,128)(2,1)S(1)}, bf16[8,64,512]{2,1,0:T(8,128)(2,1)}, u32[]{:S(2)}) copy-start(bf16[8,64,512]{2,1,0:T(8,128)(2,1)} %copy-done.35) | copy-start | bytes 1572868
  289.5 92.6 %copy-start.15 = (f32[256,1024]{1,0:T(8,128)S(1)}, f32[256,1024]{1,0:T(8,128)}, u32[]{:S(2)}) copy-start(f32[256,1024]{1,0:T(8,128)} %copy-done.14) | copy-start | bytes 3145732
  (99 other events, 349.0 us)
Sparse Core Ops, SparseCore 0:
  13.9 11.8 all-gather.12
  27.9 10.1 all-gather.8
  46.9 10.6 reduce-scatter.12
  67.3 10.8 reduce-scatter.8
  85.9 10.1 all-gather.14
  98.1 10.1 all-gather.10
  116.2 10.7 reduce-scatter.14
  136.5 10.7 reduce-scatter.10
  156.2 10.2 all-gather.20
  168.4 10.1 all-gather.16
  181.5 10.7 reduce-scatter.20
  195.1 10.7 reduce-scatter.16
  214.0 10.2 all-gather.22
  230.3 10.2 all-gather.18
  249.2 9.7 reduce-scatter.22
  268.1 9.7 reduce-scatter.18
  288.2 666.4 all-reduce.4
